TPU v7x, 32 devices: a whole 2x2x4 slice. The times are simulated.
32 devices in a mesh: cam: 8 (over z, y), proj: 4 (over x, core).
Axes of the slice: x: 2, y: 2, z: 4, core: 2. Of those that a mesh axis runs over, the one named last changes fastest.
Arguments:
- transport: bfloat16 [4096, 16384], P('cam', 'proj'), may hold values from -0.125 to 0.125
- test_panel: bfloat16 [16384, 32], P(('proj', 'cam')), may hold values from -6 to 6
Outputs:
- basis: float32 [4096, 32], P('cam')
- coimage: float32 [16384, 32], P(('proj', 'cam'))
All inputs are finite; a program needn't handle non-finite values.
Results may differ from a plain program's by a relative error of at most 0.0027.
Values may be sent and summed in bfloat16 or wider, within the bound.
A program may use at most 64 MiB of HBM per device.

v0:
```python
import jax
import jax.numpy as jnp
from jax import lax
from jax.sharding import PartitionSpec as P

ITERS = 2


def small_gram(block):
    return jnp.dot(
        block.T, block, precision=lax.Precision.HIGHEST, preferred_element_type=jnp.float32
    )


def apply_factor(gram, block):
    lower = jnp.linalg.cholesky(gram)
    return jax.scipy.linalg.solve_triangular(lower, block.T, lower=True).T


def on_device(transport, test_panel):
    rows_here = transport.shape[0]
    total_rows = rows_here * lax.axis_size("cam")
    panel_piece = test_panel
    basis = None
    coimage = None
    for step in range(ITERS):
        partial_sketch = jnp.dot(
            transport,
            lax.all_gather(panel_piece, "cam", axis=0, tiled=True),
            preferred_element_type=jnp.float32,
        )
        sketch = lax.psum(partial_sketch, "proj")
        gram = lax.psum(small_gram(sketch), "cam") / total_rows
        basis = apply_factor(gram, sketch)
        basis_low = basis.astype(jnp.bfloat16)
        last = step + 1 == ITERS
        coimage = lax.psum_scatter(
            lax.dot_general(
                transport, basis_low, (((0,), (0,)), ((), ())), preferred_element_type=jnp.float32
            ),
            "cam",
            scatter_dimension=0,
            tiled=True,
        )
        if not last:
            panel_piece = coimage.astype(jnp.bfloat16)
    return (basis, coimage)


def solution(mesh):
    placed = (P("cam", "proj"), P(("proj", "cam"), None))
    return jax.shard_map(
        on_device,
        mesh=mesh,
        in_specs=placed,
        out_specs=(P("cam", None), P(("proj", "cam"), None)),
        check_vma=False,
    )
```

profile of v0, /device:TPU:0, one launch (start us, length us, event | category | flops | bytes accessed | tf_op | source)
XLA Modules:
  0.0 366.6 jit_solution(17401557184060415915)
XLA Ops:
  7.2 32.7 %all_gather.6 = bf16[4096,32]{0,1:T(8,128)(2,1)S(1)} all-gather(bf16[512,32]{0,1:T(8,128)(2,1)} %param.6), channel_id=1, replica_groups=mesh['cam'=8,'proj'=4] {'cam'}, dimensions={0}, use_global_device_ids=true | all-gather | bytes 294912 | tf_op jit(solution)/shard_map/all_gather | solution.py:29
  39.9 4.2 %fusion.11 = f32[512,32]{0,1:T(8,128)} fusion(bf16[512,4096]{1,0:T(8,128)(2,1)} %param.5, bf16[4096,32]{0,1:T(8,128)(2,1)S(1)} %all_gather.6), kind=kOutput, calls=%fused_computation.27 | convolution fusion | flops 134217728 | bytes 4521984 | tf_op jit(solution)/shard_map/dot_general | solution.py:27
  44.2 32.1 %all-reduce.3.cloned.1.call-done = f32[512,32]{0,1:T(8,128)} async-done(((f32[512,32]{0,1:T(8,128)}), f32[512,32]{0,1:T(8,128)}) %all-reduce.3.cloned.1.call-update) | async-done | bytes 65552 | tf_op jit(solution)/shard_map/psum | solution.py:32
  76.3 1.1 fusion.12
  77.5 37.1 %psum.29 = f32[32,32]{0,1:T(8,128)S(1)} all-reduce(f32[32,32]{0,1:T(8,128)S(1)} %fusion.12), channel_id=1, replica_groups=mesh['cam'=8,'proj'=4] {'cam'}, use_global_device_ids=true, to_apply=%region_1.0 | all-reduce | flops 1024 | bytes 8192 | tf_op jit(solution)/shard_map/psum | solution.py:33
  114.6 2.9 cholesky.44
  117.6 0.6 compare_reduce_fusion.1
  118.2 0.7 fusion.3
  118.9 2.5 custom-call.6
  121.3 1.1 convolution_convert_fusion
  122.4 3.8 %convolution_bitcast_fusion.1 = f32[4096,32]{0,1:T(8,128)} fusion(bf16[32,512]{1,0:T(8,128)(2,1)S(1)} %convolution_convert_fusion, bf16[512,4096]{1,0:T(8,128)(2,1)} %param.5), kind=kOutput, calls=%fused_computation.1 | convolution fusion | flops 134217728 | bytes 4751360 | tf_op jit(solution)/shard_map/dot_general | solution.py:38
  126.3 58.8 %reduce-scatter.3.cloned.1.call-done = f32[512,32]{0,1:T(8,128)} async-done(((f32[4096,32]{0,1:T(8,128)}), f32[512,32]{0,1:T(8,128)}) %reduce-scatter.3.cloned.1.call-update) | async-done | bytes 65552 | tf_op jit(solution)/shard_map/reduce_scatter | solution.py:37
  185.1 0.8 convert_element_type.11
  185.9 30.9 %all_gather.7 = bf16[4096,32]{0,1:T(8,128)(2,1)S(1)} all-gather(bf16[512,32]{0,1:T(8,128)(2,1)S(1)} %convert_element_type.11), channel_id=1, replica_groups=mesh['cam'=8,'proj'=4] {'cam'}, dimensions={0}, use_global_device_ids=true | all-gather | bytes 294912 | tf_op jit(solution)/shard_map/all_gather | solution.py:29
  216.8 4.2 %convolution_bitcast_fusion.3 = f32[512,32]{0,1:T(8,128)} fusion(bf16[4096,32]{0,1:T(8,128)(2,1)S(1)} %all_gather.7, bf16[512,4096]{1,0:T(8,128)(2,1)} %param.5), kind=kOutput, calls=%fused_computation.3 | convolution fusion | flops 134217728 | bytes 4521984 | tf_op jit(solution)/shard_map/dot_general | solution.py:27
  221.1 30.3 %all-reduce.5.cloned.1.call-done = f32[512,32]{0,1:T(8,128)} async-done(((f32[512,32]{0,1:T(8,128)}), f32[512,32]{0,1:T(8,128)}) %all-reduce.5.cloned.1.call-update) | async-done | bytes 65552 | tf_op jit(solution)/shard_map/psum | solution.py:32
  251.3 1.1 fusion.13
  252.4 37.1 %psum.31 = f32[32,32]{0,1:T(8,128)S(1)} all-reduce(f32[32,32]{0,1:T(8,128)S(1)} %fusion.13), channel_id=1, replica_groups=mesh['cam'=8,'proj'=4] {'cam'}, use_global_device_ids=true, to_apply=%region_6.9 | all-reduce | flops 1024 | bytes 8192 | tf_op jit(solution)/shard_map/psum | solution.py:33
  289.6 2.9 cholesky.55
  293.2 0.7 fusion.4
  293.9 2.5 custom-call.7
  296.3 1.1 convolution_bitcast_fusion.2
  297.4 3.8 %convolution_bitcast_fusion = f32[4096,32]{0,1:T(8,128)} fusion(bf16[512,4096]{1,0:T(8,128)(2,1)} %param.5, f32[512,32]{0,1:T(8,128)S(1)} %convolution_bitcast_fusion.2), kind=kOutput, calls=%fused_computation | convolution fusion | flops 134234112 | bytes 4784128 | tf_op jit(solution)/shard_map/dot_general | solution.py:38
  301.3 58.8 %reduce-scatter.5.cloned.1.call-done = f32[512,32]{0,1:T(8,128)} async-done(((f32[4096,32]{0,1:T(8,128)}), f32[512,32]{0,1:T(8,128)}) %reduce-scatter.5.cloned.1.call-update) | async-done | bytes 65552 | tf_op jit(solution)/shard_map/reduce_scatter | solution.py:37
  (19 shorter events, 1.1 us)
Async XLA Ops:
  7.2 69.2 %all-reduce.3.cloned.1.call-start = ((), (), s32[]{:S(2)}) async-start(), calls=%async_computation.2 | async-start | bytes 131072 | tf_op jit(solution)/shard_map/psum | solution.py:32
  44.2 140.9 %reduce-scatter.3.cloned.1.call-start = ((), (), s32[]{:S(2)}) async-start(), calls=%async_computation.3 | async-start | bytes 589824 | tf_op jit(solution)/shard_map/reduce_scatter | solution.py:37
  126.3 125.0 %all-reduce.5.cloned.1.call-start = ((), (), s32[]{:S(2)}) async-start(), calls=%async_computation.4 | async-start | bytes 131072 | tf_op jit(solution)/shard_map/psum | solution.py:32
  221.0 139.1 %reduce-scatter.5.cloned.1.call-start = ((), (), s32[]{:S(2)}) async-start(), calls=%async_computation.5 | async-start | bytes 589824 | tf_op jit(solution)/shard_map/reduce_scatter | solution.py:37
  297.4 62.7 %copy-start = (f32[512,32]{0,1:T(8,128)}, f32[512,32]{0,1:T(8,128)S(1)}, u32[]{:S(2)}) copy-start(f32[512,32]{0,1:T(8,128)S(1)} %convolution_bitcast_fusion.2) | copy-start | bytes 196612
Sparse Core Ops, SparseCore 0:
  44.3 32.0 all-reduce.2
  126.4 58.6 reduce-scatter.2
  221.1 30.1 all-reduce.4
  301.4 58.6 reduce-scatter.4
where the time goes:
time: 367 us
  waiting for transfers between devices  180 us (49%)
  blocking collectives  138 us (38%)
  matrix products  20.4 us (6%)
  other arithmetic  14.3 us (4%)
  between operations  13.8 us (4%)
    reduce_scatter x2, waiting for transfers between devices, on_device(): lax.psum_scatter(lax.dot_general(transport, basis_low, (((0,), (0,)), (()...  118 us
    psum x2, blocking collectives, on_device(): gram = lax.psum(small_gram(sketch), 'cam') / total_rows  74.2 us
    all_gather x2, blocking collectives, on_device(): lax.all_gather(panel_piece, 'cam', axis=0, tiled=True)  63.6 us
    psum x2, waiting for transfers between devices, on_device(): sketch = lax.psum(partial_sketch, 'proj')  62.4 us
    dot_general x2, matrix products, on_device(): jnp.dot(transport, lax.all_gather(panel_piece, 'cam', axis=0, tiled=True)...  8.37 us
    dot_general x2, matrix products, on_device(): lax.dot_general(transport, basis_low, (((0,), (0,)), ((), ())), preferred...  7.64 us
  transfers between devices with their start and end apart: 4, of which 4 were waited for; matrix products, arithmetic and copies ran while one was open for 0% of the time, Pallas kernels for 0%

commit v1 on v0

v1 whole, which is shorter than its diff:
```python
import functools

import jax
import jax.numpy as jnp
from jax import lax
from jax.experimental import pallas as pl
from jax.experimental.pallas import tpu as pltpu
from jax.sharding import PartitionSpec as P

ITERS = 2
MESH = pl.DeviceIdType.MESH
HIGHEST = lax.Precision.HIGHEST
NT = (((1,), (1,)), ((), ()))


def small_gram(block):
    return jnp.dot(block.T, block, precision=HIGHEST, preferred_element_type=jnp.float32)


def apply_factor(gram, block):
    lower = jnp.linalg.cholesky(gram)
    return jax.scipy.linalg.solve_triangular(lower, block.T, lower=True).T


def with_collectives(transport, test_panel):
    total_rows = transport.shape[0] * lax.axis_size("cam")
    panel_piece = test_panel
    for step in range(ITERS):
        partial_sketch = jnp.dot(
            transport,
            lax.all_gather(panel_piece, "cam", axis=0, tiled=True),
            preferred_element_type=jnp.float32,
        )
        sketch = lax.psum(partial_sketch, "proj")
        gram = lax.psum(small_gram(sketch), "cam") / total_rows
        basis = apply_factor(gram, sketch)
        coimage = lax.psum_scatter(
            lax.dot_general(
                transport,
                basis.astype(jnp.bfloat16),
                (((0,), (0,)), ((), ())),
                preferred_element_type=jnp.float32,
            ),
            "cam",
            scatter_dimension=0,
            tiled=True,
        )
        panel_piece = coimage.astype(jnp.bfloat16)
    return basis, coimage


def inverse_factor(gram):
    size = gram.shape[0]
    row = lax.broadcasted_iota(jnp.int32, (size, size), 0)
    col = lax.broadcasted_iota(jnp.int32, (size, size), 1)
    left = gram
    right = jnp.where(row == col, 1.0, 0.0).astype(jnp.float32)
    for k in range(size):
        ratio = left[:, k : k + 1] / left[k : k + 1, k : k + 1]
        ratio = jnp.where(row[:, :1] > k, ratio, 0.0)
        right = right - ratio * right[k : k + 1, :]
        if k + 1 < size:
            left = left - ratio * left[k : k + 1, :]
    pivots = jnp.sum(jnp.where(row == col, left, 0.0), axis=1, keepdims=True)
    return right / jnp.sqrt(pivots)


def kernel(
    cams,
    projs,
    transport_ref,
    panel_ref,
    basis_ref,
    coimage_ref,
    transport,
    panels,
    partials,
    grams,
    outgoing,
    incoming,
    load_sem,
    panel_send,
    panel_recv,
    partial_send,
    partial_recv,
    gram_send,
    gram_recv,
    out_send,
    out_recv,
):
    cam, proj = lax.axis_index("cam"), lax.axis_index("proj")
    rank, piece = panel_ref.shape
    rows = transport.shape[1]

    offsets = sorted(range(1, cams), key=lambda o: -min(o, cams - o))
    cam_peers = [lax.rem(cam + o, cams) for o in offsets]
    proj_peers = [lax.rem(proj + o, projs) for o in range(1, projs)]

    loads = []
    for c in range(cams):
        load = pltpu.make_async_copy(
            transport_ref.at[:, pl.ds(c * piece, piece)], transport.at[c], load_sem.at[c]
        )
        load.start()
        loads.append(load)

    barrier = pltpu.get_barrier_semaphore()
    for peer in cam_peers:
        pl.semaphore_signal(barrier, inc=1, device_id=(peer, proj), device_id_type=MESH)
    for peer in proj_peers:
        pl.semaphore_signal(barrier, inc=1, device_id=(cam, peer), device_id_type=MESH)
    panels[0, cam] = panel_ref[...]
    pl.semaphore_wait(barrier, cams - 1 + projs - 1)

    def send(src, dst, send_sem, recv_sem, device):
        copy = pltpu.make_async_remote_copy(
            src_ref=src,
            dst_ref=dst,
            send_sem=send_sem,
            recv_sem=recv_sem,
            device_id=device,
            device_id_type=MESH,
        )
        copy.start()
        return copy

    def arrived(slot, send_sem, recv_sem, device):
        pltpu.make_async_remote_copy(
            src_ref=slot,
            dst_ref=slot,
            send_sem=send_sem,
            recv_sem=recv_sem,
            device_id=device,
            device_id_type=MESH,
        ).wait_recv()

    sends = []
    for step in range(ITERS):
        for peer in cam_peers:
            slot = panels.at[step, cam]
            sends.append(
                send(slot, slot, panel_send.at[step, peer], panel_recv.at[step, cam], (peer, proj))
            )
        if step == 0:
            for load in loads:
                load.wait()
        total = lax.dot_general(
            transport[cam], panels[step, cam], NT, preferred_element_type=jnp.float32
        )
        for peer in reversed(cam_peers):
            arrived(
                panels.at[step, peer], panel_send.at[step, peer], panel_recv.at[step, peer], (peer, proj)
            )
            total += lax.dot_general(
                transport[peer], panels[step, peer], NT, preferred_element_type=jnp.float32
            )
        row = lax.broadcasted_iota(jnp.int32, (rank, rank), 0)
        col = lax.broadcasted_iota(jnp.int32, (rank, rank), 1)
        eye = jnp.where(row == col, 1.0, 0.0).astype(jnp.float32)
        partials[step, proj] = lax.dot_general(
            eye, total, NT, precision=HIGHEST, preferred_element_type=jnp.float32
        )
        for peer in proj_peers:
            slot = partials.at[step, proj]
            sends.append(
                send(slot, slot, partial_send.at[step, peer], partial_recv.at[step, proj], (cam, peer))
            )
        for peer in proj_peers:
            arrived(
                partials.at[step, peer],
                partial_send.at[step, peer],
                partial_recv.at[step, peer],
                (cam, peer),
            )
        sketch = partials[step, 0]
        for j in range(1, projs):
            sketch += partials[step, j]

        grams[step, cam] = lax.dot_general(
            sketch, sketch, NT, precision=HIGHEST, preferred_element_type=jnp.float32
        )
        for peer in cam_peers:
            slot = grams.at[step, cam]
            sends.append(
                send(slot, slot, gram_send.at[step, peer], gram_recv.at[step, cam], (peer, proj))
            )

        high = sketch.astype(jnp.bfloat16)
        low = (sketch - high.astype(jnp.float32)).astype(jnp.bfloat16)
        both = jnp.concatenate([high, low], axis=0)

        def product(c):
            halves = jnp.dot(both, transport[c], preferred_element_type=jnp.float32)
            return halves[:rank] + halves[rank:]

        for peer in cam_peers:
            outgoing[step, peer] = product(peer)
            sends.append(
                send(
                    outgoing.at[step, peer],
                    incoming.at[step, cam],
                    out_send.at[step, peer],
                    out_recv.at[step, cam],
                    (peer, proj),
                )
            )
        summed = product(cam)

        for peer in cam_peers:
            arrived(grams.at[step, peer], gram_send.at[step, peer], gram_recv.at[step, peer], (peer, proj))
        gram = grams[step, 0]
        for c in range(1, cams):
            gram += grams[step, c]
        inverse = inverse_factor(gram / (rows * cams))
        last = step + 1 == ITERS
        if last:
            basis_ref[...] = jnp.dot(
                inverse, sketch, precision=HIGHEST, preferred_element_type=jnp.float32
            )

        for peer in reversed(cam_peers):
            arrived(incoming.at[step, peer], out_send.at[step, peer], out_recv.at[step, peer], (peer, proj))
            summed += incoming[step, peer]
        coimage = jnp.dot(inverse, summed, precision=HIGHEST, preferred_element_type=jnp.float32)
        if last:
            coimage_ref[...] = coimage
        else:
            panels[step + 1, cam] = coimage.astype(jnp.bfloat16)

    for copy in sends:
        copy.wait_send()


def with_kernel(cams, projs, transport, test_panel):
    rows, columns = transport.shape
    piece, rank = test_panel.shape
    dma = pltpu.SemaphoreType.DMA
    basis, coimage = pl.pallas_call(
        functools.partial(kernel, cams, projs),
        out_shape=(
            jax.ShapeDtypeStruct((rank, rows), jnp.float32),
            jax.ShapeDtypeStruct((rank, piece), jnp.float32),
        ),
        in_specs=[
            pl.BlockSpec(memory_space=pl.ANY),
            pl.BlockSpec(memory_space=pltpu.VMEM),
        ],
        out_specs=(
            pl.BlockSpec(memory_space=pltpu.VMEM),
            pl.BlockSpec(memory_space=pltpu.VMEM),
        ),
        scratch_shapes=[
            pltpu.VMEM((cams, rows, piece), jnp.bfloat16),
            pltpu.VMEM((ITERS, cams, rank, piece), jnp.bfloat16),
            pltpu.VMEM((ITERS, projs, rank, rows), jnp.float32),
            pltpu.VMEM((ITERS, cams, rank, rank), jnp.float32),
            pltpu.VMEM((ITERS, cams, rank, piece), jnp.float32),
            pltpu.VMEM((ITERS, cams, rank, piece), jnp.float32),
            dma((cams,)),
            dma((ITERS, cams)),
            dma((ITERS, cams)),
            dma((ITERS, projs)),
            dma((ITERS, projs)),
            dma((ITERS, cams)),
            dma((ITERS, cams)),
            dma((ITERS, cams)),
            dma((ITERS, cams)),
        ],
        compiler_params=pltpu.CompilerParams(
            collective_id=0, has_side_effects=True, vmem_limit_bytes=60 * 2**20
        ),
        cost_estimate=pl.CostEstimate(
            flops=4 * ITERS * rows * columns * rank,
            bytes_accessed=2 * rows * columns,
            transcendentals=0,
        ),
    )(transport, test_panel.T)
    return basis.T, coimage.T


def solution(mesh):
    cams, projs = mesh.shape["cam"], mesh.shape["proj"]

    def on_device(transport, test_panel):
        if test_panel.shape[0] % 128 or transport.shape[0] % 128:
            return with_collectives(transport, test_panel)
        return with_kernel(cams, projs, transport, test_panel)

    return jax.shard_map(
        on_device,
        mesh=mesh,
        in_specs=(P("cam", "proj"), P(("proj", "cam"), None)),
        out_specs=(P("cam", None), P(("proj", "cam"), None)),
        check_vma=False,
    )
```

time: 367 us -> 67.9 us (0.19)
  waiting for transfers between devices: 180 us -> 0 us
  blocking collectives: 138 us -> 0 us
  Pallas kernels: 0 us -> 63.5 us
  matrix products: 20.4 us -> 0 us
  other arithmetic: 14.3 us -> 0 us
  between operations: 13.8 us -> 0.64 us
    reduce_scatter x2 -> x0, waiting for transfers between devices: 118 us -> none  [on_device(): lax.psum_scatter(lax.dot_general(transport, basis_low, (((0,), (0,)), (()...]
    psum x2 -> x0, blocking collectives: 74.2 us -> none  [on_device(): gram = lax.psum(small_gram(sketch), 'cam') / total_rows]
    all_gather x2 -> x0, blocking collectives: 63.6 us -> none  [on_device(): lax.all_gather(panel_piece, 'cam', axis=0, tiled=True)]
    pallas_call x0 -> x1, Pallas kernels: none -> 63.5 us  [with_kernel(): pl.pallas_call(functools.partial(kernel, cams, projs), out_shape=(jax.Sha...]
    psum x2 -> x0, waiting for transfers between devices: 62.4 us -> none  [on_device(): sketch = lax.psum(partial_sketch, 'proj')]
    dot_general x6 -> x0, matrix products: 18.2 us -> none  [the longest x2 8.37 us: on_device(): jnp.dot(transport, lax.all_gather(panel_piece, 'cam', axis=0, tiled=True)...]
    another operation x10 -> x0, other arithmetic: 13.4 us -> none  [the longest x6 7.19 us: apply_factor(): lower = jnp.linalg.cholesky(gram)]
  transfers between devices with their start and end apart: 4 -> 0, of which waited for: 4 -> 0; matrix products, arithmetic and copies ran while one was open for 0% -> 0% of each run, Pallas kernels for 0% -> 0%
where the time goes in v1:
time: 67.9 us; the launch traced here: 67.1 us
  Pallas kernels  63.5 us (94%)
  local copies, waits for them, and re-layouts  2.95 us (4%)
    pallas_call x1, Pallas kernels, with_kernel(): pl.pallas_call(functools.partial(kernel, cams, projs), out_shape=(jax.Sha...  63.5 us
    unnamed x2, local copies, waits for them, and re-layouts  2.95 us

profile of v1, /device:TPU:0, one launch (start us, length us, event | category | flops | bytes accessed | tf_op | source)
XLA Modules:
  0.0 67.1 jit_solution(13080284826134707058)
XLA Ops:
  0.6 63.5 %shard_map.41 = (f32[32,512]{1,0:T(8,128)}, f32[32,512]{1,0:T(8,128)}) custom-call(bf16[512,4096]{1,0:T(8,128)(2,1)} %transport_ref.1, bf16[32,512]{1,0:T(8,128)(2,1)} %bitcast.5), custom_call_target="tpu_custom_call" | custom-call | flops 536870912 | bytes 4194304 | tf_op jit(solution)/shard_map/pallas_call | solution.py:238
  64.2 1.5 %copy.6 = f32[512,32]{0,1:T(8,128)} copy(f32[512,32]{0,1:T(8,128)} %bitcast.4) | data formatting | bytes 131072
  65.7 1.5 %copy.7 = f32[512,32]{0,1:T(8,128)} copy(f32[512,32]{0,1:T(8,128)} %bitcast.3) | data formatting | bytes 131072

commit v2 on v1

v2 whole, which is shorter than its diff:
```python
import functools

import jax
import jax.numpy as jnp
from jax import lax
from jax.experimental import pallas as pl
from jax.experimental.pallas import tpu as pltpu
from jax.sharding import PartitionSpec as P

ITERS = 2
MESH = pl.DeviceIdType.MESH
HIGHEST = lax.Precision.HIGHEST
NT = (((1,), (1,)), ((), ()))


def small_gram(block):
    return jnp.dot(block.T, block, precision=HIGHEST, preferred_element_type=jnp.float32)


def apply_factor(gram, block):
    lower = jnp.linalg.cholesky(gram)
    return jax.scipy.linalg.solve_triangular(lower, block.T, lower=True).T


def with_collectives(transport, test_panel):
    total_rows = transport.shape[0] * lax.axis_size("cam")
    panel_piece = test_panel
    for step in range(ITERS):
        partial_sketch = jnp.dot(
            transport,
            lax.all_gather(panel_piece, "cam", axis=0, tiled=True),
            preferred_element_type=jnp.float32,
        )
        sketch = lax.psum(partial_sketch, "proj")
        gram = lax.psum(small_gram(sketch), "cam") / total_rows
        basis = apply_factor(gram, sketch)
        coimage = lax.psum_scatter(
            lax.dot_general(
                transport,
                basis.astype(jnp.bfloat16),
                (((0,), (0,)), ((), ())),
                preferred_element_type=jnp.float32,
            ),
            "cam",
            scatter_dimension=0,
            tiled=True,
        )
        panel_piece = coimage.astype(jnp.bfloat16)
    return basis, coimage


def inverse_factor(gram):
    size = gram.shape[0]
    row = lax.broadcasted_iota(jnp.int32, (size, size), 0)
    col = lax.broadcasted_iota(jnp.int32, (size, size), 1)
    left = gram
    right = jnp.where(row == col, 1.0, 0.0).astype(jnp.float32)
    for k in range(size):
        ratio = left[:, k : k + 1] / left[k : k + 1, k : k + 1]
        ratio = jnp.where(row[:, :1] > k, ratio, 0.0)
        right = right - ratio * right[k : k + 1, :]
        if k + 1 < size:
            left = left - ratio * left[k : k + 1, :]
    pivots = jnp.sum(jnp.where(row == col, left, 0.0), axis=1, keepdims=True)
    return right / jnp.sqrt(pivots)


def kernel(
    cams,
    projs,
    transport_ref,
    panel_ref,
    basis_ref,
    coimage_ref,
    transport,
    panels,
    partials,
    grams,
    pair_out,
    pair_in,
    line_out,
    line_in,
    load_sem,
    panel_send,
    panel_recv,
    partial_send,
    partial_recv,
    gram_send,
    gram_recv,
    pair_send,
    pair_recv,
    line_send,
    line_recv,
):
    cam, proj = lax.axis_index("cam"), lax.axis_index("proj")
    rank, piece = panel_ref.shape
    rows = transport.shape[1]

    spots = cams // 2
    spot, side = cam // 2, lax.rem(cam, 2)
    other = 1 - side
    pair = 2 * spot + other
    offsets = sorted(range(1, spots), key=lambda o: -min(o, spots - o))
    line = [lax.rem(spot + o, spots) for o in offsets]
    cam_peers = [lax.rem(cam + o, cams) for o in range(1, cams)]
    proj_peers = [lax.rem(proj + o, projs) for o in range(1, projs)]

    loads = []
    for c in range(cams):
        load = pltpu.make_async_copy(
            transport_ref.at[:, pl.ds(c * piece, piece)], transport.at[c], load_sem.at[c]
        )
        load.start()
        loads.append(load)

    barrier = pltpu.get_barrier_semaphore()
    for peer in cam_peers:
        pl.semaphore_signal(barrier, inc=1, device_id=(peer, proj), device_id_type=MESH)
    for peer in proj_peers:
        pl.semaphore_signal(barrier, inc=1, device_id=(cam, peer), device_id_type=MESH)
    panels[0, cam] = panel_ref[...]
    pl.semaphore_wait(barrier, cams - 1 + projs - 1)

    sends = []

    def send(src, dst, send_sem, recv_sem, device):
        copy = pltpu.make_async_remote_copy(
            src_ref=src,
            dst_ref=dst,
            send_sem=send_sem,
            recv_sem=recv_sem,
            device_id=device,
            device_id_type=MESH,
        )
        copy.start()
        sends.append(copy)

    def arrived(slot, send_sem, recv_sem):
        pltpu.make_async_remote_copy(
            src_ref=slot,
            dst_ref=slot,
            send_sem=send_sem,
            recv_sem=recv_sem,
            device_id=(pair, proj),
            device_id_type=MESH,
        ).wait_recv()

    for step in range(ITERS):

        def share(c, peer, sem):
            slot = panels.at[step, c]
            send(slot, slot, panel_send.at[step, sem], panel_recv.at[step, c], (peer, proj))

        def sketched(c):
            return lax.dot_general(
                transport[c], panels[step, c], NT, preferred_element_type=jnp.float32
            )

        def wait_panel(c):
            arrived(panels.at[step, c], panel_send.at[step, c], panel_recv.at[step, c])

        for s in line:
            share(cam, 2 * s + side, 2 * s + side)
        share(cam, pair, pair)
        if step == 0:
            for load in loads:
                load.wait()
        total = sketched(cam)
        for s in reversed(line):
            wait_panel(2 * s + side)
            share(2 * s + side, pair, 2 * s + other)
            total += sketched(2 * s + side)
        wait_panel(pair)
        total += sketched(pair)
        for s in reversed(line):
            wait_panel(2 * s + other)
            total += sketched(2 * s + other)

        row = lax.broadcasted_iota(jnp.int32, (rank, rank), 0)
        col = lax.broadcasted_iota(jnp.int32, (rank, rank), 1)
        eye = jnp.where(row == col, 1.0, 0.0).astype(jnp.float32)
        partials[step, proj] = lax.dot_general(
            eye, total, NT, precision=HIGHEST, preferred_element_type=jnp.float32
        )
        for peer in proj_peers:
            slot = partials.at[step, proj]
            send(slot, slot, partial_send.at[step, peer], partial_recv.at[step, proj], (cam, peer))
        for peer in proj_peers:
            arrived(partials.at[step, peer], partial_send.at[step, peer], partial_recv.at[step, peer])
        sketch = partials[step, 0]
        for j in range(1, projs):
            sketch += partials[step, j]

        high = sketch.astype(jnp.bfloat16)
        low = (sketch - high.astype(jnp.float32)).astype(jnp.bfloat16)
        both = jnp.concatenate([high, low], axis=0)

        def product(c):
            halves = jnp.dot(both, transport[c], preferred_element_type=jnp.float32)
            return halves[:rank] + halves[rank:]

        def to_pair(s):
            pair_out[step, s] = product(2 * s + other)
            send(
                pair_out.at[step, s],
                pair_in.at[step, s],
                pair_send.at[step, s],
                pair_recv.at[step, s],
                (pair, proj),
            )

        def from_pair(s):
            arrived(pair_in.at[step, s], pair_send.at[step, s], pair_recv.at[step, s])
            return pair_in[step, s]

        to_pair(line[0])
        gram = lax.dot_general(
            sketch, sketch, NT, precision=HIGHEST, preferred_element_type=jnp.float32
        )
        folds = 128 // rank
        tall = rank // folds
        grams[step, cam] = jnp.concatenate(
            [gram[f * tall : (f + 1) * tall] for f in range(folds)], axis=1
        )
        for peer in cam_peers:
            slot = grams.at[step, cam]
            send(slot, slot, gram_send.at[step, peer], gram_recv.at[step, cam], (peer, proj))
        for s in line[1:] + [spot]:
            to_pair(s)
        for s in line:
            mine = product(2 * s + side)
            line_out[step, s] = mine + from_pair(s)
            send(
                line_out.at[step, s],
                line_in.at[step, spot],
                line_send.at[step, s],
                line_recv.at[step, spot],
                (2 * s + side, proj),
            )
        summed = product(cam) + from_pair(spot)

        for peer in cam_peers:
            arrived(grams.at[step, peer], gram_send.at[step, peer], gram_recv.at[step, peer])
        folded = grams[step, 0]
        for c in range(1, cams):
            folded += grams[step, c]
        folded = folded / (rows * cams)
        inverse = inverse_factor(
            jnp.concatenate([folded[:, f * rank : (f + 1) * rank] for f in range(folds)], axis=0)
        )
        last = step + 1 == ITERS
        if last:
            basis_ref[...] = jnp.dot(
                inverse, sketch, precision=HIGHEST, preferred_element_type=jnp.float32
            )

        for s in reversed(line):
            arrived(line_in.at[step, s], line_send.at[step, s], line_recv.at[step, s])
            summed += line_in[step, s]
        coimage = jnp.dot(inverse, summed, precision=HIGHEST, preferred_element_type=jnp.float32)
        if last:
            coimage_ref[...] = coimage
        else:
            panels[step + 1, cam] = coimage.astype(jnp.bfloat16)

    for copy in sends:
        copy.wait_send()


def deliver(basis_ref, coimage_ref, basis_out, coimage_out, sem):
    first = pltpu.make_async_copy(basis_ref, basis_out, sem.at[0])
    second = pltpu.make_async_copy(coimage_ref, coimage_out, sem.at[1])
    first.start()
    second.start()
    first.wait()
    second.wait()


def with_kernel(cams, projs, transport, test_panel):
    rows, columns = transport.shape
    piece, rank = test_panel.shape
    dma = pltpu.SemaphoreType.DMA
    in_vmem = pl.BlockSpec(memory_space=pltpu.VMEM)
    anywhere = pl.BlockSpec(memory_space=pl.ANY)
    results = (
        jax.ShapeDtypeStruct((rank, rows), jnp.float32),
        jax.ShapeDtypeStruct((rank, piece), jnp.float32),
    )
    exchanged = pltpu.VMEM((ITERS, cams // 2, rank, piece), jnp.float32)
    basis, coimage = pl.pallas_call(
        functools.partial(kernel, cams, projs),
        out_shape=results,
        in_specs=[anywhere, in_vmem],
        out_specs=(in_vmem, in_vmem),
        scratch_shapes=[
            pltpu.VMEM((cams, rows, piece), jnp.bfloat16),
            pltpu.VMEM((ITERS, cams, rank, piece), jnp.bfloat16),
            pltpu.VMEM((ITERS, projs, rank, rows), jnp.float32),
            pltpu.VMEM((ITERS, cams, rank * rank // 128, 128), jnp.float32),
            exchanged,
            exchanged,
            exchanged,
            exchanged,
            dma((cams,)),
            dma((ITERS, cams)),
            dma((ITERS, cams)),
            dma((ITERS, projs)),
            dma((ITERS, projs)),
            dma((ITERS, cams)),
            dma((ITERS, cams)),
            dma((ITERS, cams // 2)),
            dma((ITERS, cams // 2)),
            dma((ITERS, cams // 2)),
            dma((ITERS, cams // 2)),
        ],
        compiler_params=pltpu.CompilerParams(
            collective_id=0, has_side_effects=True, vmem_limit_bytes=60 * 2**20
        ),
        cost_estimate=pl.CostEstimate(
            flops=4 * ITERS * rows * columns * rank,
            bytes_accessed=2 * rows * columns,
            transcendentals=0,
        ),
    )(transport, test_panel.T)
    basis, coimage = pl.pallas_call(
        deliver,
        out_shape=results,
        in_specs=[anywhere, anywhere],
        out_specs=(anywhere, anywhere),
        scratch_shapes=[dma((2,))],
    )(basis, coimage)
    return basis.T, coimage.T


def solution(mesh):
    cams, projs = mesh.shape["cam"], mesh.shape["proj"]

    def on_device(transport, test_panel):
        if test_panel.shape[0] % 128 or transport.shape[0] % 128 or cams % 2:
            return with_collectives(transport, test_panel)
        return with_kernel(cams, projs, transport, test_panel)

    return jax.shard_map(
        on_device,
        mesh=mesh,
        in_specs=(P("cam", "proj"), P(("proj", "cam"), None)),
        out_specs=(P("cam", None), P(("proj", "cam"), None)),
        check_vma=False,
    )
```

time: 67.9 us -> 62.1 us (0.915)
  local copies, waits for them, and re-layouts: 2.95 us -> 0 us
  Pallas kernels: 63.5 us -> 61.3 us
    unnamed x2 -> x0, local copies, waits for them, and re-layouts: 2.95 us -> none
    pallas_call x1 -> x2, Pallas kernels: 63.5 us -> 61.3 us  [the longest x1 56.2 us: with_kernel(): pl.pallas_call(functools.partial(kernel, cams, projs), out_shape=results,...]
where the time goes in v2:
time: 62.1 us; the launch traced here: 61.9 us
  Pallas kernels  61.3 us (99%)
  between operations  0.64 us (1%)
    pallas_call x1, Pallas kernels, with_kernel(): pl.pallas_call(functools.partial(kernel, cams, projs), out_shape=results,...  56.2 us
    pallas_call x1, Pallas kernels, with_kernel(): pl.pallas_call(deliver, out_shape=results, in_specs=[anywhere, anywhere],...  5.09 us

profile of v2, /device:TPU:0, one launch (start us, length us, event | category | flops | bytes accessed | tf_op | source)
XLA Modules:
  0.0 61.9 jit_solution(5960584474802517132)
XLA Ops:
  0.6 56.2 %shard_map.41 = (f32[32,512]{1,0:T(8,128)}, f32[32,512]{1,0:T(8,128)}) custom-call(bf16[512,4096]{1,0:T(8,128)(2,1)} %transport_ref.1, bf16[32,512]{1,0:T(8,128)(2,1)} %bitcast.3), custom_call_target="tpu_custom_call" | custom-call | flops 536870912 | bytes 4194304 | tf_op jit(solution)/shard_map/pallas_call | solution.py:290
  56.8 5.1 %shard_map.42 = (f32[32,512]{1,0:T(8,128)}, f32[32,512]{1,0:T(8,128)}) custom-call(f32[32,512]{1,0:T(8,128)} %get-tuple-element.6.basis_ref, f32[32,512]{1,0:T(8,128)} %get-tuple-element.7.coimage_ref), custom_call_target="tpu_custom_call" | custom-call | tf_op jit(solution)/shard_map/pallas_call | solution.py:325

commit v3 on v2

--- a/solution.py
+++ b/solution.py
@@ -8,6 +8,7 @@
 from jax.sharding import PartitionSpec as P
 
 ITERS = 2
+HALVES = 2
 MESH = pl.DeviceIdType.MESH
 HIGHEST = lax.Precision.HIGHEST
 NT = (((1,), (1,)), ((), ()))
@@ -118,7 +119,8 @@
         pl.semaphore_signal(barrier, inc=1, device_id=(peer, proj), device_id_type=MESH)
     for peer in proj_peers:
         pl.semaphore_signal(barrier, inc=1, device_id=(cam, peer), device_id_type=MESH)
-    panels[0, cam] = panel_ref[...]
+    for i in range(HALVES):
+        panels[i, cam] = panel_ref[i * (rank // HALVES) : (i + 1) * (rank // HALVES), :]
     pl.semaphore_wait(barrier, cams - 1 + projs - 1)
 
     sends = []
@@ -145,75 +147,101 @@
             device_id_type=MESH,
         ).wait_recv()
 
+    width = rank // HALVES
+    row = lax.broadcasted_iota(jnp.int32, (width, width), 0)
+    col = lax.broadcasted_iota(jnp.int32, (width, width), 1)
+    eye = jnp.where(row == col, 1.0, 0.0).astype(jnp.float32)
+
+    def share(q, c, peer, sem):
+        slot = panels.at[q, c]
+        send(slot, slot, panel_send.at[q, sem], panel_recv.at[q, c], (peer, proj))
+
+    def wait_panel(q, c):
+        arrived(panels.at[q, c], panel_send.at[q, c], panel_recv.at[q, c])
+
+    def sketched(q, c):
+        return lax.dot_general(
+            transport[c], panels[q, c], NT, preferred_element_type=jnp.float32
+        )
+
+    def product(both, c):
+        halves = jnp.dot(both, transport[c], preferred_element_type=jnp.float32)
+        return halves[:width] + halves[width:]
+
+    def to_pair(q, both, s):
+        pair_out[q, s] = product(both, 2 * s + other)
+        send(
+            pair_out.at[q, s],
+            pair_in.at[q, s],
+            pair_send.at[q, s],
+            pair_recv.at[q, s],
+            (pair, proj),
+        )
+
+    def from_pair(q, s):
+        arrived(pair_in.at[q, s], pair_send.at[q, s], pair_recv.at[q, s])
+        return pair_in[q, s]
+
+    def to_line(q, both, s):
+        line_out[q, s] = product(both, 2 * s + side) + from_pair(q, s)
+        send(
+            line_out.at[q, s],
+            line_in.at[q, spot],
+            line_send.at[q, s],
+            line_recv.at[q, spot],
+            (2 * s + side, proj),
+        )
+
     for step in range(ITERS):
-
-        def share(c, peer, sem):
-            slot = panels.at[step, c]
-            send(slot, slot, panel_send.at[step, sem], panel_recv.at[step, c], (peer, proj))
-
-        def sketched(c):
-            return lax.dot_general(
-                transport[c], panels[step, c], NT, preferred_element_type=jnp.float32
-            )
-
-        def wait_panel(c):
-            arrived(panels.at[step, c], panel_send.at[step, c], panel_recv.at[step, c])
-
-        for s in line:
-            share(cam, 2 * s + side, 2 * s + side)
-        share(cam, pair, pair)
+        parts = range(step * HALVES, (step + 1) * HALVES)
+        for q in parts:
+            for s in line:
+                share(q, cam, 2 * s + side, 2 * s + side)
+            share(q, cam, pair, pair)
         if step == 0:
             for load in loads:
                 load.wait()
-        total = sketched(cam)
-        for s in reversed(line):
-            wait_panel(2 * s + side)
-            share(2 * s + side, pair, 2 * s + other)
-            total += sketched(2 * s + side)
-        wait_panel(pair)
-        total += sketched(pair)
-        for s in reversed(line):
-            wait_panel(2 * s + other)
-            total += sketched(2 * s + other)
-
-        row = lax.broadcasted_iota(jnp.int32, (rank, rank), 0)
-        col = lax.broadcasted_iota(jnp.int32, (rank, rank), 1)
-        eye = jnp.where(row == col, 1.0, 0.0).astype(jnp.float32)
-        partials[step, proj] = lax.dot_general(
-            eye, total, NT, precision=HIGHEST, preferred_element_type=jnp.float32
-        )
-        for peer in proj_peers:
-            slot = partials.at[step, proj]
-            send(slot, slot, partial_send.at[step, peer], partial_recv.at[step, proj], (cam, peer))
-        for peer in proj_peers:
-            arrived(partials.at[step, peer], partial_send.at[step, peer], partial_recv.at[step, peer])
-        sketch = partials[step, 0]
-        for j in range(1, projs):
-            sketch += partials[step, j]
-
-        high = sketch.astype(jnp.bfloat16)
-        low = (sketch - high.astype(jnp.float32)).astype(jnp.bfloat16)
-        both = jnp.concatenate([high, low], axis=0)
-
-        def product(c):
-            halves = jnp.dot(both, transport[c], preferred_element_type=jnp.float32)
-            return halves[:rank] + halves[rank:]
-
-        def to_pair(s):
-            pair_out[step, s] = product(2 * s + other)
-            send(
-                pair_out.at[step, s],
-                pair_in.at[step, s],
-                pair_send.at[step, s],
-                pair_recv.at[step, s],
-                (pair, proj),
+        totals = []
+        for q in parts:
+            total = sketched(q, cam)
+            for s in reversed(line):
+                wait_panel(q, 2 * s + side)
+                share(q, 2 * s + side, pair, 2 * s + other)
+                total += sketched(q, 2 * s + side)
+            totals.append(total)
+        for q, total in zip(parts, totals):
+            wait_panel(q, pair)
+            total += sketched(q, pair)
+            for s in reversed(line):
+                wait_panel(q, 2 * s + other)
+                total += sketched(q, 2 * s + other)
+            partials[q, proj] = lax.dot_general(
+                eye, total, NT, precision=HIGHEST, preferred_element_type=jnp.float32
             )
-
-        def from_pair(s):
-            arrived(pair_in.at[step, s], pair_send.at[step, s], pair_recv.at[step, s])
-            return pair_in[step, s]
-
-        to_pair(line[0])
+            for peer in proj_peers:
+                slot = partials.at[q, proj]
+                send(slot, slot, partial_send.at[q, peer], partial_recv.at[q, proj], (cam, peer))
+
+        sketches = []
+        split = []
+        for q in parts:
+            for peer in proj_peers:
+                arrived(partials.at[q, peer], partial_send.at[q, peer], partial_recv.at[q, peer])
+            sketch = partials[q, 0]
+            for j in range(1, projs):
+                sketch += partials[q, j]
+            high = sketch.astype(jnp.bfloat16)
+            low = (sketch - high.astype(jnp.float32)).astype(jnp.bfloat16)
+            sketches.append(sketch)
+            split.append(jnp.concatenate([high, low], axis=0))
+            for s in line + [spot]:
+                to_pair(q, split[-1], s)
+                if len(split) > 1 and s is not spot:
+                    to_line(q - 1, split[-2], s)
+        for s in line:
+            to_line(parts[-1], split[-1], s)
+
+        sketch = jnp.concatenate(sketches, axis=0)
         gram = lax.dot_general(
             sketch, sketch, NT, precision=HIGHEST, preferred_element_type=jnp.float32
         )
@@ -225,19 +253,7 @@
         for peer in cam_peers:
             slot = grams.at[step, cam]
             send(slot, slot, gram_send.at[step, peer], gram_recv.at[step, cam], (peer, proj))
-        for s in line[1:] + [spot]:
-            to_pair(s)
-        for s in line:
-            mine = product(2 * s + side)
-            line_out[step, s] = mine + from_pair(s)
-            send(
-                line_out.at[step, s],
-                line_in.at[step, spot],
-                line_send.at[step, s],
-                line_recv.at[step, spot],
-                (2 * s + side, proj),
-            )
-        summed = product(cam) + from_pair(spot)
+        sums = [product(both, cam) + from_pair(q, spot) for q, both in zip(parts, split)]
 
         for peer in cam_peers:
             arrived(grams.at[step, peer], gram_send.at[step, peer], gram_recv.at[step, peer])
@@ -254,26 +270,44 @@
                 inverse, sketch, precision=HIGHEST, preferred_element_type=jnp.float32
             )
 
-        for s in reversed(line):
-            arrived(line_in.at[step, s], line_send.at[step, s], line_recv.at[step, s])
-            summed += line_in[step, s]
-        coimage = jnp.dot(inverse, summed, precision=HIGHEST, preferred_element_type=jnp.float32)
+        for i, q in enumerate(parts):
+            for s in reversed(line):
+                arrived(line_in.at[q, s], line_send.at[q, s], line_recv.at[q, s])
+                sums[i] += line_in[q, s]
+        coimage = jnp.dot(
+            inverse,
+            jnp.concatenate(sums, axis=0),
+            precision=HIGHEST,
+            preferred_element_type=jnp.float32,
+        )
         if last:
             coimage_ref[...] = coimage
         else:
-            panels[step + 1, cam] = coimage.astype(jnp.bfloat16)
+            for i in range(HALVES):
+                panels[parts[-1] + 1 + i, cam] = coimage[i * width : (i + 1) * width].astype(
+                    jnp.bfloat16
+                )
 
     for copy in sends:
         copy.wait_send()
 
 
-def deliver(basis_ref, coimage_ref, basis_out, coimage_out, sem):
-    first = pltpu.make_async_copy(basis_ref, basis_out, sem.at[0])
-    second = pltpu.make_async_copy(coimage_ref, coimage_out, sem.at[1])
-    first.start()
-    second.start()
-    first.wait()
-    second.wait()
+def deliver(basis_ref, coimage_ref, basis_out, coimage_out, basis, coimage, sem):
+    reads = [
+        pltpu.make_async_copy(basis_ref, basis, sem.at[0]),
+        pltpu.make_async_copy(coimage_ref, coimage, sem.at[1]),
+    ]
+    writes = [
+        pltpu.make_async_copy(basis, basis_out, sem.at[2]),
+        pltpu.make_async_copy(coimage, coimage_out, sem.at[3]),
+    ]
+    for read in reads:
+        read.start()
+    for read, write in zip(reads, writes):
+        read.wait()
+        write.start()
+    for write in writes:
+        write.wait()
 
 
 def with_kernel(cams, projs, transport, test_panel):
@@ -286,7 +320,9 @@
         jax.ShapeDtypeStruct((rank, rows), jnp.float32),
         jax.ShapeDtypeStruct((rank, piece), jnp.float32),
     )
-    exchanged = pltpu.VMEM((ITERS, cams // 2, rank, piece), jnp.float32)
+    width = rank // HALVES
+    parts = ITERS * HALVES
+    exchanged = pltpu.VMEM((parts, cams // 2, width, piece), jnp.float32)
     basis, coimage = pl.pallas_call(
         functools.partial(kernel, cams, projs),
         out_shape=results,
@@ -294,24 +330,24 @@
         out_specs=(in_vmem, in_vmem),
         scratch_shapes=[
             pltpu.VMEM((cams, rows, piece), jnp.bfloat16),
-            pltpu.VMEM((ITERS, cams, rank, piece), jnp.bfloat16),
-            pltpu.VMEM((ITERS, projs, rank, rows), jnp.float32),
+            pltpu.VMEM((parts, cams, width, piece), jnp.bfloat16),
+            pltpu.VMEM((parts, projs, width, rows), jnp.float32),
             pltpu.VMEM((ITERS, cams, rank * rank // 128, 128), jnp.float32),
             exchanged,
             exchanged,
             exchanged,
             exchanged,
             dma((cams,)),
+            dma((parts, cams)),
+            dma((parts, cams)),
+            dma((parts, projs)),
+            dma((parts, projs)),
             dma((ITERS, cams)),
             dma((ITERS, cams)),
-            dma((ITERS, projs)),
-            dma((ITERS, projs)),
-            dma((ITERS, cams)),
-            dma((ITERS, cams)),
-            dma((ITERS, cams // 2)),
-            dma((ITERS, cams // 2)),
-            dma((ITERS, cams // 2)),
-            dma((ITERS, cams // 2)),
+            dma((parts, cams // 2)),
+            dma((parts, cams // 2)),
+            dma((parts, cams // 2)),
+            dma((parts, cams // 2)),
         ],
         compiler_params=pltpu.CompilerParams(
             collective_id=0, has_side_effects=True, vmem_limit_bytes=60 * 2**20
@@ -327,7 +363,11 @@
         out_shape=results,
         in_specs=[anywhere, anywhere],
         out_specs=(anywhere, anywhere),
-        scratch_shapes=[dma((2,))],
+        scratch_shapes=[
+            pltpu.VMEM((rank, rows), jnp.float32),
+            pltpu.VMEM((rank, piece), jnp.float32),
+            dma((4,)),
+        ],
     )(basis, coimage)
     return basis.T, coimage.T
 

time: 62.1 us -> 63 us (1.014)
  Pallas kernels: 61.3 us -> 62.1 us
    pallas_call x1, Pallas kernels: 56.2 us -> 60.6 us  [with_kernel(): pl.pallas_call(functools.partial(kernel, cams, projs), out_shape=results,...]
    pallas_call x1, Pallas kernels: 5.09 us -> 1.53 us  [with_kernel(): pl.pallas_call(deliver, out_shape=results, in_specs=[anywhere, anywhere],...]
where the time goes in v3:
time: 63 us; the launch traced here: 62.8 us
  Pallas kernels  62.1 us (99%)
  between operations  0.64 us (1%)
    pallas_call x1, Pallas kernels, with_kernel(): pl.pallas_call(functools.partial(kernel, cams, projs), out_shape=results,...  60.6 us
    pallas_call x1, Pallas kernels, with_kernel(): pl.pallas_call(deliver, out_shape=results, in_specs=[anywhere, anywhere],...  1.53 us

profile of v3, /device:TPU:0, one launch (start us, length us, event | category | flops | bytes accessed | tf_op | source)
XLA Modules:
  0.0 62.8 jit_solution(4196195981667123221)
XLA Ops:
  0.6 60.6 %shard_map.41 = (f32[32,512]{1,0:T(8,128)}, f32[32,512]{1,0:T(8,128)}) custom-call(bf16[512,4096]{1,0:T(8,128)(2,1)} %transport_ref.1, bf16[32,512]{1,0:T(8,128)(2,1)} %bitcast.3), custom_call_target="tpu_custom_call" | custom-call | flops 536870912 | bytes 4194304 | tf_op jit(solution)/shard_map/pallas_call | solution.py:326
  61.2 1.5 %shard_map.42 = (f32[32,512]{1,0:T(8,128)}, f32[32,512]{1,0:T(8,128)}) custom-call(f32[32,512]{1,0:T(8,128)} %get-tuple-element.6.basis_ref, f32[32,512]{1,0:T(8,128)} %get-tuple-element.7.coimage_ref), custom_call_target="tpu_custom_call" | custom-call | tf_op jit(solution)/shard_map/pallas_call | solution.py:361

commit v4 on v2

--- a/solution.py
+++ b/solution.py
@@ -121,10 +121,8 @@
     panels[0, cam] = panel_ref[...]
     pl.semaphore_wait(barrier, cams - 1 + projs - 1)
 
-    sends = []
-
-    def send(src, dst, send_sem, recv_sem, device):
-        copy = pltpu.make_async_remote_copy(
+    def copy_of(src, dst, send_sem, recv_sem, device):
+        return pltpu.make_async_remote_copy(
             src_ref=src,
             dst_ref=dst,
             send_sem=send_sem,
@@ -132,39 +130,42 @@
             device_id=device,
             device_id_type=MESH,
         )
-        copy.start()
-        sends.append(copy)
 
     def arrived(slot, send_sem, recv_sem):
-        pltpu.make_async_remote_copy(
-            src_ref=slot,
-            dst_ref=slot,
-            send_sem=send_sem,
-            recv_sem=recv_sem,
-            device_id=(pair, proj),
-            device_id_type=MESH,
-        ).wait_recv()
-
-    for step in range(ITERS):
+        copy_of(slot, slot, send_sem, recv_sem, (pair, proj)).wait_recv()
+
+    folds = 128 // rank
+    tall = rank // folds
+
+    def one_pass(step, carry):
+        sends = []
+
+        def send(*parts):
+            copy = copy_of(*parts)
+            copy.start()
+            sends.append(copy)
 
         def share(c, peer, sem):
             slot = panels.at[step, c]
             send(slot, slot, panel_send.at[step, sem], panel_recv.at[step, c], (peer, proj))
 
+        def wait_panel(c):
+            arrived(panels.at[step, c], panel_send.at[step, c], panel_recv.at[step, c])
+
         def sketched(c):
             return lax.dot_general(
-                transport[c], panels[step, c], NT, preferred_element_type=jnp.float32
+                panels[step, c], transport[c], NT, preferred_element_type=jnp.float32
             )
-
-        def wait_panel(c):
-            arrived(panels.at[step, c], panel_send.at[step, c], panel_recv.at[step, c])
 
         for s in line:
             share(cam, 2 * s + side, 2 * s + side)
         share(cam, pair, pair)
-        if step == 0:
+
+        @pl.when(step == 0)
+        def _():
             for load in loads:
                 load.wait()
+
         total = sketched(cam)
         for s in reversed(line):
             wait_panel(2 * s + side)
@@ -175,13 +176,7 @@
         for s in reversed(line):
             wait_panel(2 * s + other)
             total += sketched(2 * s + other)
-
-        row = lax.broadcasted_iota(jnp.int32, (rank, rank), 0)
-        col = lax.broadcasted_iota(jnp.int32, (rank, rank), 1)
-        eye = jnp.where(row == col, 1.0, 0.0).astype(jnp.float32)
-        partials[step, proj] = lax.dot_general(
-            eye, total, NT, precision=HIGHEST, preferred_element_type=jnp.float32
-        )
+        partials[step, proj] = total
         for peer in proj_peers:
             slot = partials.at[step, proj]
             send(slot, slot, partial_send.at[step, peer], partial_recv.at[step, proj], (cam, peer))
@@ -213,23 +208,20 @@
             arrived(pair_in.at[step, s], pair_send.at[step, s], pair_recv.at[step, s])
             return pair_in[step, s]
 
-        to_pair(line[0])
+        for s in line:
+            to_pair(s)
         gram = lax.dot_general(
             sketch, sketch, NT, precision=HIGHEST, preferred_element_type=jnp.float32
         )
-        folds = 128 // rank
-        tall = rank // folds
         grams[step, cam] = jnp.concatenate(
             [gram[f * tall : (f + 1) * tall] for f in range(folds)], axis=1
         )
         for peer in cam_peers:
             slot = grams.at[step, cam]
             send(slot, slot, gram_send.at[step, peer], gram_recv.at[step, cam], (peer, proj))
-        for s in line[1:] + [spot]:
-            to_pair(s)
+        to_pair(spot)
         for s in line:
-            mine = product(2 * s + side)
-            line_out[step, s] = mine + from_pair(s)
+            line_out[step, s] = product(2 * s + side) + from_pair(s)
             send(
                 line_out.at[step, s],
                 line_in.at[step, spot],
@@ -248,32 +240,39 @@
         inverse = inverse_factor(
             jnp.concatenate([folded[:, f * rank : (f + 1) * rank] for f in range(folds)], axis=0)
         )
-        last = step + 1 == ITERS
-        if last:
-            basis_ref[...] = jnp.dot(
-                inverse, sketch, precision=HIGHEST, preferred_element_type=jnp.float32
-            )
+        basis_ref[...] = jnp.dot(
+            inverse, sketch, precision=HIGHEST, preferred_element_type=jnp.float32
+        )
 
         for s in reversed(line):
             arrived(line_in.at[step, s], line_send.at[step, s], line_recv.at[step, s])
             summed += line_in[step, s]
         coimage = jnp.dot(inverse, summed, precision=HIGHEST, preferred_element_type=jnp.float32)
-        if last:
-            coimage_ref[...] = coimage
-        else:
-            panels[step + 1, cam] = coimage.astype(jnp.bfloat16)
-
-    for copy in sends:
-        copy.wait_send()
-
-
-def deliver(basis_ref, coimage_ref, basis_out, coimage_out, sem):
-    first = pltpu.make_async_copy(basis_ref, basis_out, sem.at[0])
-    second = pltpu.make_async_copy(coimage_ref, coimage_out, sem.at[1])
-    first.start()
-    second.start()
-    first.wait()
-    second.wait()
+        coimage_ref[...] = coimage
+        panels[step + 1, cam] = coimage.astype(jnp.bfloat16)
+        for copy in sends:
+            copy.wait_send()
+        return carry
+
+    lax.fori_loop(0, ITERS, one_pass, 0)
+
+
+def deliver(basis_ref, coimage_ref, basis_out, coimage_out, basis, coimage, sem):
+    reads = [
+        pltpu.make_async_copy(basis_ref, basis, sem.at[0]),
+        pltpu.make_async_copy(coimage_ref, coimage, sem.at[1]),
+    ]
+    writes = [
+        pltpu.make_async_copy(basis, basis_out, sem.at[2]),
+        pltpu.make_async_copy(coimage, coimage_out, sem.at[3]),
+    ]
+    for read in reads:
+        read.start()
+    for read, write in zip(reads, writes):
+        read.wait()
+        write.start()
+    for write in writes:
+        write.wait()
 
 
 def with_kernel(cams, projs, transport, test_panel):
@@ -294,7 +293,7 @@
         out_specs=(in_vmem, in_vmem),
         scratch_shapes=[
             pltpu.VMEM((cams, rows, piece), jnp.bfloat16),
-            pltpu.VMEM((ITERS, cams, rank, piece), jnp.bfloat16),
+            pltpu.VMEM((ITERS + 1, cams, rank, piece), jnp.bfloat16),
             pltpu.VMEM((ITERS, projs, rank, rows), jnp.float32),
             pltpu.VMEM((ITERS, cams, rank * rank // 128, 128), jnp.float32),
             exchanged,
@@ -327,7 +326,11 @@
         out_shape=results,
         in_specs=[anywhere, anywhere],
         out_specs=(anywhere, anywhere),
-        scratch_shapes=[dma((2,))],
+        scratch_shapes=[
+            pltpu.VMEM((rank, rows), jnp.float32),
+            pltpu.VMEM((rank, piece), jnp.float32),
+            dma((4,)),
+        ],
     )(basis, coimage)
     return basis.T, coimage.T
 

time: 62.1 us -> 57.4 us (0.924)
  Pallas kernels: 61.3 us -> 56.5 us
    pallas_call x1, Pallas kernels: 5.09 us -> 1.53 us  [with_kernel(): pl.pallas_call(deliver, out_shape=results, in_specs=[anywhere, anywhere],...]
    pallas_call x1, Pallas kernels: 56.2 us -> 55 us  [with_kernel(): pl.pallas_call(functools.partial(kernel, cams, projs), out_shape=results,...]
where the time goes in v4:
time: 57.4 us; the launch traced here: 57.1 us
  Pallas kernels  56.5 us (98%)
  between operations  0.64 us (1%)
    pallas_call x1, Pallas kernels, with_kernel(): pl.pallas_call(functools.partial(kernel, cams, projs), out_shape=results,...  55 us
    pallas_call x1, Pallas kernels, with_kernel(): pl.pallas_call(deliver, out_shape=results, in_specs=[anywhere, anywhere],...  1.53 us

profile of v4, /device:TPU:0, one launch (start us, length us, event | category | flops | bytes accessed | tf_op | source)
XLA Modules:
  0.0 57.1 jit_solution(14296999264454512756)
XLA Ops:
  0.6 55.0 %shard_map.41 = (f32[32,512]{1,0:T(8,128)}, f32[32,512]{1,0:T(8,128)}) custom-call(bf16[512,4096]{1,0:T(8,128)(2,1)} %transport_ref.1, bf16[32,512]{1,0:T(8,128)(2,1)} %bitcast.3), custom_call_target="tpu_custom_call" | custom-call | flops 536870912 | bytes 4194304 | tf_op jit(solution)/shard_map/pallas_call | solution.py:289
  55.6 1.5 %shard_map.42 = (f32[32,512]{1,0:T(8,128)}, f32[32,512]{1,0:T(8,128)}) custom-call(f32[32,512]{1,0:T(8,128)} %get-tuple-element.6.basis_ref, f32[32,512]{1,0:T(8,128)} %get-tuple-element.7.coimage_ref), custom_call_target="tpu_custom_call" | custom-call | tf_op jit(solution)/shard_map/pallas_call | solution.py:324

commit v5 on v4

--- a/solution.py
+++ b/solution.py
@@ -49,18 +49,19 @@
     return basis, coimage
 
 
-def inverse_factor(gram):
-    size = gram.shape[0]
-    row = lax.broadcasted_iota(jnp.int32, (size, size), 0)
-    col = lax.broadcasted_iota(jnp.int32, (size, size), 1)
-    left = gram
-    right = jnp.where(row == col, 1.0, 0.0).astype(jnp.float32)
-    for k in range(size):
+def eliminate(left, right, start, stop):
+    row = lax.broadcasted_iota(jnp.int32, (left.shape[0], 1), 0)
+    for k in range(start, stop):
         ratio = left[:, k : k + 1] / left[k : k + 1, k : k + 1]
-        ratio = jnp.where(row[:, :1] > k, ratio, 0.0)
+        ratio = jnp.where(row > k, ratio, 0.0)
         right = right - ratio * right[k : k + 1, :]
-        if k + 1 < size:
-            left = left - ratio * left[k : k + 1, :]
+        left = left - ratio * left[k : k + 1, :]
+    return left, right
+
+
+def inverse_factor(left, right):
+    row = lax.broadcasted_iota(jnp.int32, left.shape, 0)
+    col = lax.broadcasted_iota(jnp.int32, left.shape, 1)
     pivots = jnp.sum(jnp.where(row == col, left, 0.0), axis=1, keepdims=True)
     return right / jnp.sqrt(pivots)
 
@@ -208,8 +209,7 @@
             arrived(pair_in.at[step, s], pair_send.at[step, s], pair_recv.at[step, s])
             return pair_in[step, s]
 
-        for s in line:
-            to_pair(s)
+        to_pair(line[0])
         gram = lax.dot_general(
             sketch, sketch, NT, precision=HIGHEST, preferred_element_type=jnp.float32
         )
@@ -219,8 +219,11 @@
         for peer in cam_peers:
             slot = grams.at[step, cam]
             send(slot, slot, gram_send.at[step, peer], gram_recv.at[step, cam], (peer, proj))
-        to_pair(spot)
-        for s in line:
+        for s in line[1:] + [spot]:
+            to_pair(s)
+
+        done = 0
+        for i, s in enumerate(line):
             line_out[step, s] = product(2 * s + side) + from_pair(s)
             send(
                 line_out.at[step, s],
@@ -229,17 +232,24 @@
                 line_recv.at[step, spot],
                 (2 * s + side, proj),
             )
+            if i == 0:
+                for peer in cam_peers:
+                    arrived(grams.at[step, peer], gram_send.at[step, peer], gram_recv.at[step, peer])
+                folded = grams[step, 0]
+                for c in range(1, cams):
+                    folded += grams[step, c]
+                folded = folded / (rows * cams)
+                left = jnp.concatenate(
+                    [folded[:, f * rank : (f + 1) * rank] for f in range(folds)], axis=0
+                )
+                row = lax.broadcasted_iota(jnp.int32, (rank, rank), 0)
+                col = lax.broadcasted_iota(jnp.int32, (rank, rank), 1)
+                right = jnp.where(row == col, 1.0, 0.0).astype(jnp.float32)
+            upto = rank * (i + 1) // len(line)
+            left, right = eliminate(left, right, done, upto)
+            done = upto
+        inverse = inverse_factor(left, right)
         summed = product(cam) + from_pair(spot)
-
-        for peer in cam_peers:
-            arrived(grams.at[step, peer], gram_send.at[step, peer], gram_recv.at[step, peer])
-        folded = grams[step, 0]
-        for c in range(1, cams):
-            folded += grams[step, c]
-        folded = folded / (rows * cams)
-        inverse = inverse_factor(
-            jnp.concatenate([folded[:, f * rank : (f + 1) * rank] for f in range(folds)], axis=0)
-        )
         basis_ref[...] = jnp.dot(
             inverse, sketch, precision=HIGHEST, preferred_element_type=jnp.float32
         )
@@ -339,7 +349,7 @@
     cams, projs = mesh.shape["cam"], mesh.shape["proj"]
 
     def on_device(transport, test_panel):
-        if test_panel.shape[0] % 128 or transport.shape[0] % 128 or cams % 2:
+        if test_panel.shape[0] % 128 or transport.shape[0] % 128 or cams % 2 or cams < 4:
             return with_collectives(transport, test_panel)
         return with_kernel(cams, projs, transport, test_panel)
 

time: 57.4 us -> 57.9 us (level)
  Pallas kernels: 56.5 us -> 57.1 us
where the time goes in v5:
time: 57.9 us; the launch traced here: 57.7 us
  Pallas kernels  57.1 us (99%)
  between operations  0.64 us (1%)
    pallas_call x1, Pallas kernels, with_kernel(): pl.pallas_call(functools.partial(kernel, cams, projs), out_shape=results,...  55.5 us
    pallas_call x1, Pallas kernels, with_kernel(): pl.pallas_call(deliver, out_shape=results, in_specs=[anywhere, anywhere],...  1.53 us

profile of v5, /device:TPU:0, one launch (start us, length us, event | category | flops | bytes accessed | tf_op | source)
XLA Modules:
  0.0 57.7 jit_solution(7766204173619711482)
XLA Ops:
  0.6 55.5 %shard_map.41 = (f32[32,512]{1,0:T(8,128)}, f32[32,512]{1,0:T(8,128)}) custom-call(bf16[512,4096]{1,0:T(8,128)(2,1)} %transport_ref.1, bf16[32,512]{1,0:T(8,128)(2,1)} %bitcast.3), custom_call_target="tpu_custom_call" | custom-call | flops 536870912 | bytes 4194304 | tf_op jit(solution)/shard_map/pallas_call | solution.py:299
  56.2 1.5 %shard_map.42 = (f32[32,512]{1,0:T(8,128)}, f32[32,512]{1,0:T(8,128)}) custom-call(f32[32,512]{1,0:T(8,128)} %get-tuple-element.6.basis_ref, f32[32,512]{1,0:T(8,128)} %get-tuple-element.7.coimage_ref), custom_call_target="tpu_custom_call" | custom-call | tf_op jit(solution)/shard_map/pallas_call | solution.py:334

commit v6 on v5

--- a/solution.py
+++ b/solution.py
@@ -76,6 +76,7 @@
     transport,
     panels,
     partials,
+    duos,
     grams,
     pair_out,
     pair_in,
@@ -86,6 +87,8 @@
     panel_recv,
     partial_send,
     partial_recv,
+    duo_send,
+    duo_recv,
     gram_send,
     gram_recv,
     pair_send,
@@ -104,7 +107,10 @@
     offsets = sorted(range(1, spots), key=lambda o: -min(o, spots - o))
     line = [lax.rem(spot + o, spots) for o in offsets]
     cam_peers = [lax.rem(cam + o, cams) for o in range(1, cams)]
-    proj_peers = [lax.rem(proj + o, projs) for o in range(1, projs)]
+    duo, core = proj // 2, lax.rem(proj, 2)
+    sibling = 2 * duo + 1 - core
+    other_duos = [lax.rem(duo + o, projs // 2) for o in range(1, projs // 2)]
+    proj_peers = [sibling] + [2 * d + core for d in other_duos]
 
     loads = []
     for c in range(cams):
@@ -120,7 +126,7 @@
     for peer in proj_peers:
         pl.semaphore_signal(barrier, inc=1, device_id=(cam, peer), device_id_type=MESH)
     panels[0, cam] = panel_ref[...]
-    pl.semaphore_wait(barrier, cams - 1 + projs - 1)
+    pl.semaphore_wait(barrier, cams - 1 + projs // 2)
 
     def copy_of(src, dst, send_sem, recv_sem, device):
         return pltpu.make_async_remote_copy(
@@ -177,15 +183,19 @@
         for s in reversed(line):
             wait_panel(2 * s + other)
             total += sketched(2 * s + other)
-        partials[step, proj] = total
-        for peer in proj_peers:
-            slot = partials.at[step, proj]
-            send(slot, slot, partial_send.at[step, peer], partial_recv.at[step, proj], (cam, peer))
-        for peer in proj_peers:
-            arrived(partials.at[step, peer], partial_send.at[step, peer], partial_recv.at[step, peer])
-        sketch = partials[step, 0]
-        for j in range(1, projs):
-            sketch += partials[step, j]
+        partials[step, core] = total
+        slot = partials.at[step, core]
+        send(slot, slot, partial_send.at[step, 0], partial_recv.at[step, 0], (cam, sibling))
+        arrived(partials.at[step, 1 - core], partial_send.at[step, 0], partial_recv.at[step, 0])
+        duos[step, duo] = partials[step, 0] + partials[step, 1]
+        for d in other_duos:
+            slot = duos.at[step, duo]
+            send(slot, slot, duo_send.at[step, d], duo_recv.at[step, duo], (cam, 2 * d + core))
+        for d in other_duos:
+            arrived(duos.at[step, d], duo_send.at[step, d], duo_recv.at[step, d])
+        sketch = duos[step, 0]
+        for d in range(1, projs // 2):
+            sketch += duos[step, d]
 
         high = sketch.astype(jnp.bfloat16)
         low = (sketch - high.astype(jnp.float32)).astype(jnp.bfloat16)
@@ -222,8 +232,7 @@
         for s in line[1:] + [spot]:
             to_pair(s)
 
-        done = 0
-        for i, s in enumerate(line):
+        for s in line:
             line_out[step, s] = product(2 * s + side) + from_pair(s)
             send(
                 line_out.at[step, s],
@@ -232,22 +241,19 @@
                 line_recv.at[step, spot],
                 (2 * s + side, proj),
             )
-            if i == 0:
-                for peer in cam_peers:
-                    arrived(grams.at[step, peer], gram_send.at[step, peer], gram_recv.at[step, peer])
-                folded = grams[step, 0]
-                for c in range(1, cams):
-                    folded += grams[step, c]
-                folded = folded / (rows * cams)
-                left = jnp.concatenate(
-                    [folded[:, f * rank : (f + 1) * rank] for f in range(folds)], axis=0
-                )
-                row = lax.broadcasted_iota(jnp.int32, (rank, rank), 0)
-                col = lax.broadcasted_iota(jnp.int32, (rank, rank), 1)
-                right = jnp.where(row == col, 1.0, 0.0).astype(jnp.float32)
-            upto = rank * (i + 1) // len(line)
-            left, right = eliminate(left, right, done, upto)
-            done = upto
+        for peer in cam_peers:
+            arrived(grams.at[step, peer], gram_send.at[step, peer], gram_recv.at[step, peer])
+        folded = grams[step, 0]
+        for c in range(1, cams):
+            folded += grams[step, c]
+        folded = folded / (rows * cams)
+        left = jnp.concatenate(
+            [folded[:, f * rank : (f + 1) * rank] for f in range(folds)], axis=0
+        )
+        row = lax.broadcasted_iota(jnp.int32, (rank, rank), 0)
+        col = lax.broadcasted_iota(jnp.int32, (rank, rank), 1)
+        identity = jnp.where(row == col, 1.0, 0.0).astype(jnp.float32)
+        left, right = eliminate(left, identity, 0, rank)
         inverse = inverse_factor(left, right)
         summed = product(cam) + from_pair(spot)
         basis_ref[...] = jnp.dot(
@@ -304,7 +310,8 @@
         scratch_shapes=[
             pltpu.VMEM((cams, rows, piece), jnp.bfloat16),
             pltpu.VMEM((ITERS + 1, cams, rank, piece), jnp.bfloat16),
-            pltpu.VMEM((ITERS, projs, rank, rows), jnp.float32),
+            pltpu.VMEM((ITERS, 2, rank, rows), jnp.float32),
+            pltpu.VMEM((ITERS, projs // 2, rank, rows), jnp.float32),
             pltpu.VMEM((ITERS, cams, rank * rank // 128, 128), jnp.float32),
             exchanged,
             exchanged,
@@ -313,8 +320,10 @@
             dma((cams,)),
             dma((ITERS, cams)),
             dma((ITERS, cams)),
-            dma((ITERS, projs)),
-            dma((ITERS, projs)),
+            dma((ITERS, 1)),
+            dma((ITERS, 1)),
+            dma((ITERS, projs // 2)),
+            dma((ITERS, projs // 2)),
             dma((ITERS, cams)),
             dma((ITERS, cams)),
             dma((ITERS, cams // 2)),
@@ -349,7 +358,7 @@
     cams, projs = mesh.shape["cam"], mesh.shape["proj"]
 
     def on_device(transport, test_panel):
-        if test_panel.shape[0] % 128 or transport.shape[0] % 128 or cams % 2 or cams < 4:
+        if test_panel.shape[0] % 128 or transport.shape[0] % 128 or cams % 2 or projs % 2:
             return with_collectives(transport, test_panel)
         return with_kernel(cams, projs, transport, test_panel)
 

time: 57.9 us -> 56.4 us (0.974)
  Pallas kernels: 57.1 us -> 55.6 us
    pallas_call x1, Pallas kernels: 55.5 us -> 54 us  [with_kernel(): pl.pallas_call(functools.partial(kernel, cams, projs), out_shape=results,...]
where the time goes in v6:
time: 56.4 us; the launch traced here: 56.2 us
  Pallas kernels  55.6 us (99%)
  between operations  0.64 us (1%)
    pallas_call x1, Pallas kernels, with_kernel(): pl.pallas_call(functools.partial(kernel, cams, projs), out_shape=results,...  54 us
    pallas_call x1, Pallas kernels, with_kernel(): pl.pallas_call(deliver, out_shape=results, in_specs=[anywhere, anywhere],...  1.53 us

profile of v6, /device:TPU:0, one launch (start us, length us, event | category | flops | bytes accessed | tf_op | source)
XLA Modules:
  0.0 56.2 jit_solution(18326576884339740830)
XLA Ops:
  0.6 54.0 %shard_map.41 = (f32[32,512]{1,0:T(8,128)}, f32[32,512]{1,0:T(8,128)}) custom-call(bf16[512,4096]{1,0:T(8,128)(2,1)} %transport_ref.1, bf16[32,512]{1,0:T(8,128)(2,1)} %bitcast.3), custom_call_target="tpu_custom_call" | custom-call | flops 536870912 | bytes 4194304 | tf_op jit(solution)/shard_map/pallas_call | solution.py:305
  54.7 1.5 %shard_map.42 = (f32[32,512]{1,0:T(8,128)}, f32[32,512]{1,0:T(8,128)}) custom-call(f32[32,512]{1,0:T(8,128)} %get-tuple-element.6.basis_ref, f32[32,512]{1,0:T(8,128)} %get-tuple-element.7.coimage_ref), custom_call_target="tpu_custom_call" | custom-call | tf_op jit(solution)/shard_map/pallas_call | solution.py:343

commit v7 on v6

--- a/solution.py
+++ b/solution.py
@@ -273,19 +273,12 @@
     lax.fori_loop(0, ITERS, one_pass, 0)
 
 
-def deliver(basis_ref, coimage_ref, basis_out, coimage_out, basis, coimage, sem):
-    reads = [
-        pltpu.make_async_copy(basis_ref, basis, sem.at[0]),
-        pltpu.make_async_copy(coimage_ref, coimage, sem.at[1]),
+def deliver(basis_ref, coimage_ref, basis_out, coimage_out, sem):
+    writes = [
+        pltpu.make_async_copy(basis_ref, basis_out, sem.at[0]),
+        pltpu.make_async_copy(coimage_ref, coimage_out, sem.at[1]),
     ]
-    writes = [
-        pltpu.make_async_copy(basis, basis_out, sem.at[2]),
-        pltpu.make_async_copy(coimage, coimage_out, sem.at[3]),
-    ]
-    for read in reads:
-        read.start()
-    for read, write in zip(reads, writes):
-        read.wait()
+    for write in writes:
         write.start()
     for write in writes:
         write.wait()
@@ -301,10 +294,11 @@
         jax.ShapeDtypeStruct((rank, rows), jnp.float32),
         jax.ShapeDtypeStruct((rank, piece), jnp.float32),
     )
+    kept = (pltpu.VMEM((rank, rows), jnp.float32), pltpu.VMEM((rank, piece), jnp.float32))
     exchanged = pltpu.VMEM((ITERS, cams // 2, rank, piece), jnp.float32)
     basis, coimage = pl.pallas_call(
         functools.partial(kernel, cams, projs),
-        out_shape=results,
+        out_shape=kept,
         in_specs=[anywhere, in_vmem],
         out_specs=(in_vmem, in_vmem),
         scratch_shapes=[
@@ -343,13 +337,9 @@
     basis, coimage = pl.pallas_call(
         deliver,
         out_shape=results,
-        in_specs=[anywhere, anywhere],
+        in_specs=[in_vmem, in_vmem],
         out_specs=(anywhere, anywhere),
-        scratch_shapes=[
-            pltpu.VMEM((rank, rows), jnp.float32),
-            pltpu.VMEM((rank, piece), jnp.float32),
-            dma((4,)),
-        ],
+        scratch_shapes=[dma((2,))],
     )(basis, coimage)
     return basis.T, coimage.T
 

time: 56.4 us -> 57 us (1.011)
  local copies, waits for them, and re-layouts: 0 us -> 1.23 us
  Pallas kernels: 55.6 us -> 54.9 us
    unnamed x0 -> x4, local copies, waits for them, and re-layouts: none -> 1.23 us
    pallas_call x2, Pallas kernels: 55.6 us -> 54.9 us  [the longest x1 53.4 us: with_kernel(): pl.pallas_call(functools.partial(kernel, cams, projs), out_shape=kept, in...]
where the time goes in v7:
time: 57 us; the launch traced here: 56.8 us
  Pallas kernels  54.9 us (96%)
  local copies, waits for them, and re-layouts  1.23 us (2%)
  between operations  0.65 us (1%)
    pallas_call x1, Pallas kernels, with_kernel(): pl.pallas_call(functools.partial(kernel, cams, projs), out_shape=kept, in...  53.4 us
    pallas_call x1, Pallas kernels, with_kernel(): pl.pallas_call(deliver, out_shape=results, in_specs=[in_vmem, in_vmem], o...  1.54 us
    unnamed x4, local copies, waits for them, and re-layouts  1.23 us

profile of v7, /device:TPU:0, one launch (start us, length us, event | category | flops | bytes accessed | tf_op | source)
XLA Modules:
  0.0 56.8 jit_solution(3298199062582626005)
XLA Ops:
  0.6 53.4 %shard_map.41 = (f32[32,512]{1,0:T(8,128)S(1)}, f32[32,512]{1,0:T(8,128)S(1)}) custom-call(bf16[512,4096]{1,0:T(8,128)(2,1)} %transport_ref.1, bf16[32,512]{1,0:T(8,128)(2,1)} %bitcast.3), custom_call_target="tpu_custom_call" | custom-call | flops 536870912 | bytes 4194304 | tf_op jit(solution)/shard_map/pallas_call | solution.py:299
  54.0 0.0 copy-start
  54.1 0.6 %copy-done = f32[32,512]{1,0:T(8,128)} copy-done((f32[32,512]{1,0:T(8,128)}, f32[32,512]{1,0:T(8,128)S(1)}, u32[]{:S(2)}) %copy-start) | copy-done | bytes 65560
  54.7 0.0 copy-start.1
  54.7 0.6 %copy-done.1 = f32[32,512]{1,0:T(8,128)} copy-done((f32[32,512]{1,0:T(8,128)}, f32[32,512]{1,0:T(8,128)S(1)}, u32[]{:S(2)}) %copy-start.1) | copy-done | bytes 65560
  55.3 1.5 %shard_map.42 = (f32[32,512]{1,0:T(8,128)}, f32[32,512]{1,0:T(8,128)}) custom-call(f32[32,512]{1,0:T(8,128)} %copy-done, f32[32,512]{1,0:T(8,128)} %copy-done.1), custom_call_target="tpu_custom_call" | custom-call | tf_op jit(solution)/shard_map/pallas_call | solution.py:337
Async XLA Ops:
  54.0 0.6 %copy-start = (f32[32,512]{1,0:T(8,128)}, f32[32,512]{1,0:T(8,128)S(1)}, u32[]{:S(2)}) copy-start(f32[32,512]{1,0:T(8,128)S(1)} %get-tuple-element.6.basis_ref) | copy-start | bytes 196612
  54.7 0.6 %copy-start.1 = (f32[32,512]{1,0:T(8,128)}, f32[32,512]{1,0:T(8,128)S(1)}, u32[]{:S(2)}) copy-start(f32[32,512]{1,0:T(8,128)S(1)} %get-tuple-element.7.coimage_ref) | copy-start | bytes 196612

commit v8 on v7

--- a/solution.py
+++ b/solution.py
@@ -8,6 +8,7 @@
 from jax.sharding import PartitionSpec as P
 
 ITERS = 2
+CUTS = 2
 MESH = pl.DeviceIdType.MESH
 HIGHEST = lax.Precision.HIGHEST
 NT = (((1,), (1,)), ((), ()))
@@ -99,6 +100,7 @@
     cam, proj = lax.axis_index("cam"), lax.axis_index("proj")
     rank, piece = panel_ref.shape
     rows = transport.shape[1]
+    width = piece // CUTS
 
     spots = cams // 2
     spot, side = cam // 2, lax.rem(cam, 2)
@@ -201,23 +203,25 @@
         low = (sketch - high.astype(jnp.float32)).astype(jnp.bfloat16)
         both = jnp.concatenate([high, low], axis=0)
 
-        def product(c):
-            halves = jnp.dot(both, transport[c], preferred_element_type=jnp.float32)
+        def product(c, h):
+            block = transport[c, :, h * width : (h + 1) * width]
+            halves = jnp.dot(both, block, preferred_element_type=jnp.float32)
             return halves[:rank] + halves[rank:]
 
         def to_pair(s):
-            pair_out[step, s] = product(2 * s + other)
-            send(
-                pair_out.at[step, s],
-                pair_in.at[step, s],
-                pair_send.at[step, s],
-                pair_recv.at[step, s],
-                (pair, proj),
-            )
-
-        def from_pair(s):
-            arrived(pair_in.at[step, s], pair_send.at[step, s], pair_recv.at[step, s])
-            return pair_in[step, s]
+            for h in range(CUTS):
+                pair_out[step, s, h] = product(2 * s + other, h)
+                send(
+                    pair_out.at[step, s, h],
+                    pair_in.at[step, s, h],
+                    pair_send.at[step, s, h],
+                    pair_recv.at[step, s, h],
+                    (pair, proj),
+                )
+
+        def from_pair(s, h):
+            arrived(pair_in.at[step, s, h], pair_send.at[step, s, h], pair_recv.at[step, s, h])
+            return pair_in[step, s, h]
 
         to_pair(line[0])
         gram = lax.dot_general(
@@ -233,14 +237,15 @@
             to_pair(s)
 
         for s in line:
-            line_out[step, s] = product(2 * s + side) + from_pair(s)
-            send(
-                line_out.at[step, s],
-                line_in.at[step, spot],
-                line_send.at[step, s],
-                line_recv.at[step, spot],
-                (2 * s + side, proj),
-            )
+            for h in range(CUTS):
+                line_out[step, s, h] = product(2 * s + side, h) + from_pair(s, h)
+                send(
+                    line_out.at[step, s, h],
+                    line_in.at[step, spot, h],
+                    line_send.at[step, s, h],
+                    line_recv.at[step, spot, h],
+                    (2 * s + side, proj),
+                )
         for peer in cam_peers:
             arrived(grams.at[step, peer], gram_send.at[step, peer], gram_recv.at[step, peer])
         folded = grams[step, 0]
@@ -255,14 +260,16 @@
         identity = jnp.where(row == col, 1.0, 0.0).astype(jnp.float32)
         left, right = eliminate(left, identity, 0, rank)
         inverse = inverse_factor(left, right)
-        summed = product(cam) + from_pair(spot)
+        sums = [product(cam, h) + from_pair(spot, h) for h in range(CUTS)]
         basis_ref[...] = jnp.dot(
             inverse, sketch, precision=HIGHEST, preferred_element_type=jnp.float32
         )
 
-        for s in reversed(line):
-            arrived(line_in.at[step, s], line_send.at[step, s], line_recv.at[step, s])
-            summed += line_in[step, s]
+        for h in range(CUTS):
+            for s in line:
+                arrived(line_in.at[step, s, h], line_send.at[step, s, h], line_recv.at[step, s, h])
+                sums[h] += line_in[step, s, h]
+        summed = jnp.concatenate(sums, axis=1)
         coimage = jnp.dot(inverse, summed, precision=HIGHEST, preferred_element_type=jnp.float32)
         coimage_ref[...] = coimage
         panels[step + 1, cam] = coimage.astype(jnp.bfloat16)
@@ -290,12 +297,10 @@
     dma = pltpu.SemaphoreType.DMA
     in_vmem = pl.BlockSpec(memory_space=pltpu.VMEM)
     anywhere = pl.BlockSpec(memory_space=pl.ANY)
-    results = (
-        jax.ShapeDtypeStruct((rank, rows), jnp.float32),
-        jax.ShapeDtypeStruct((rank, piece), jnp.float32),
-    )
+    in_hbm = pl.BlockSpec(memory_space=pltpu.HBM)
+    results = (pltpu.HBM((rank, rows), jnp.float32), pltpu.HBM((rank, piece), jnp.float32))
     kept = (pltpu.VMEM((rank, rows), jnp.float32), pltpu.VMEM((rank, piece), jnp.float32))
-    exchanged = pltpu.VMEM((ITERS, cams // 2, rank, piece), jnp.float32)
+    exchanged = pltpu.VMEM((ITERS, cams // 2, CUTS, rank, piece // CUTS), jnp.float32)
     basis, coimage = pl.pallas_call(
         functools.partial(kernel, cams, projs),
         out_shape=kept,
@@ -320,10 +325,10 @@
             dma((ITERS, projs // 2)),
             dma((ITERS, cams)),
             dma((ITERS, cams)),
-            dma((ITERS, cams // 2)),
-            dma((ITERS, cams // 2)),
-            dma((ITERS, cams // 2)),
-            dma((ITERS, cams // 2)),
+            dma((ITERS, cams // 2, CUTS)),
+            dma((ITERS, cams // 2, CUTS)),
+            dma((ITERS, cams // 2, CUTS)),
+            dma((ITERS, cams // 2, CUTS)),
         ],
         compiler_params=pltpu.CompilerParams(
             collective_id=0, has_side_effects=True, vmem_limit_bytes=60 * 2**20
@@ -338,7 +343,7 @@
         deliver,
         out_shape=results,
         in_specs=[in_vmem, in_vmem],
-        out_specs=(anywhere, anywhere),
+        out_specs=(in_hbm, in_hbm),
         scratch_shapes=[dma((2,))],
     )(basis, coimage)
     return basis.T, coimage.T
@@ -348,7 +353,7 @@
     cams, projs = mesh.shape["cam"], mesh.shape["proj"]
 
     def on_device(transport, test_panel):
-        if test_panel.shape[0] % 128 or transport.shape[0] % 128 or cams % 2 or projs % 2:
+        if test_panel.shape[0] % (128 * CUTS) or transport.shape[0] % 128 or cams % 2 or projs % 2:
             return with_collectives(transport, test_panel)
         return with_kernel(cams, projs, transport, test_panel)
 

time: 57 us -> 56.2 us (0.986)
  Pallas kernels: 54.9 us -> 54.1 us
    pallas_call x1, Pallas kernels: 53.4 us -> 52.5 us  [with_kernel(): pl.pallas_call(functools.partial(kernel, cams, projs), out_shape=kept, in...]
where the time goes in v8:
time: 56.2 us; the launch traced here: 55.9 us
  Pallas kernels  54.1 us (96%)
  local copies, waits for them, and re-layouts  1.23 us (2%)
  between operations  0.65 us (1%)
    pallas_call x1, Pallas kernels, with_kernel(): pl.pallas_call(functools.partial(kernel, cams, projs), out_shape=kept, in...  52.5 us
    pallas_call x1, Pallas kernels, with_kernel(): pl.pallas_call(deliver, out_shape=results, in_specs=[in_vmem, in_vmem], o...  1.54 us
    unnamed x4, local copies, waits for them, and re-layouts  1.23 us

profile of v8, /device:TPU:0, one launch (start us, length us, event | category | flops | bytes accessed | tf_op | source)
XLA Modules:
  0.0 55.9 jit_solution(16797705206223499416)
XLA Ops:
  0.6 52.5 %shard_map.41 = (f32[32,512]{1,0:T(8,128)S(1)}, f32[32,512]{1,0:T(8,128)S(1)}) custom-call(bf16[512,4096]{1,0:T(8,128)(2,1)} %transport_ref.1, bf16[32,512]{1,0:T(8,128)(2,1)} %bitcast.3), custom_call_target="tpu_custom_call" | custom-call | flops 536870912 | bytes 4194304 | tf_op jit(solution)/shard_map/pallas_call | solution.py:304
  53.2 0.0 copy-start
  53.2 0.6 %copy-done = f32[32,512]{1,0:T(8,128)} copy-done((f32[32,512]{1,0:T(8,128)}, f32[32,512]{1,0:T(8,128)S(1)}, u32[]{:S(2)}) %copy-start) | copy-done | bytes 65560
  53.8 0.0 copy-start.1
  53.8 0.6 %copy-done.1 = f32[32,512]{1,0:T(8,128)} copy-done((f32[32,512]{1,0:T(8,128)}, f32[32,512]{1,0:T(8,128)S(1)}, u32[]{:S(2)}) %copy-start.1) | copy-done | bytes 65560
  54.4 1.5 %shard_map.42 = (f32[32,512]{1,0:T(8,128)}, f32[32,512]{1,0:T(8,128)}) custom-call(f32[32,512]{1,0:T(8,128)} %copy-done, f32[32,512]{1,0:T(8,128)} %copy-done.1), custom_call_target="tpu_custom_call" | custom-call | tf_op jit(solution)/shard_map/pallas_call | solution.py:342
Async XLA Ops:
  53.2 0.6 %copy-start = (f32[32,512]{1,0:T(8,128)}, f32[32,512]{1,0:T(8,128)S(1)}, u32[]{:S(2)}) copy-start(f32[32,512]{1,0:T(8,128)S(1)} %get-tuple-element.6.basis_ref) | copy-start | bytes 196612
  53.8 0.6 %copy-start.1 = (f32[32,512]{1,0:T(8,128)}, f32[32,512]{1,0:T(8,128)S(1)}, u32[]{:S(2)}) copy-start(f32[32,512]{1,0:T(8,128)S(1)} %get-tuple-element.7.coimage_ref) | copy-start | bytes 196612

commit v9 on v8

--- a/solution.py
+++ b/solution.py
@@ -345,6 +345,7 @@
         in_specs=[in_vmem, in_vmem],
         out_specs=(in_hbm, in_hbm),
         scratch_shapes=[dma((2,))],
+        compiler_params=pltpu.CompilerParams(vmem_limit_bytes=2**20),
     )(basis, coimage)
     return basis.T, coimage.T
 

time: 56.2 us -> 54 us (0.961)
  local copies, waits for them, and re-layouts: 1.23 us -> 0 us
  Pallas kernels: 54.1 us -> 53.2 us
    unnamed x4 -> x0, local copies, waits for them, and re-layouts: 1.23 us -> none
    pallas_call x1, Pallas kernels: 1.54 us -> 0.67 us  [with_kernel(): pl.pallas_call(deliver, out_shape=results, in_specs=[in_vmem, in_vmem], o...]
where the time goes in v9:
time: 54 us; the launch traced here: 53.8 us
  Pallas kernels  53.2 us (99%)
  between operations  0.64 us (1%)
    pallas_call x1, Pallas kernels, with_kernel(): pl.pallas_call(functools.partial(kernel, cams, projs), out_shape=kept, in...  52.5 us

profile of v9, /device:TPU:0, one launch (start us, length us, event | category | flops | bytes accessed | tf_op | source)
XLA Modules:
  0.0 53.8 jit_solution(4940491024876969607)
XLA Ops:
  0.6 52.5 %shard_map.41 = (f32[32,512]{1,0:T(8,128)S(1)}, f32[32,512]{1,0:T(8,128)S(1)}) custom-call(bf16[512,4096]{1,0:T(8,128)(2,1)} %transport_ref.1, bf16[32,512]{1,0:T(8,128)(2,1)} %bitcast.3), custom_call_target="tpu_custom_call" | custom-call | flops 536870912 | bytes 4194304 | tf_op jit(solution)/shard_map/pallas_call | solution.py:304
  53.2 0.7 %shard_map.42 = (f32[32,512]{1,0:T(8,128)}, f32[32,512]{1,0:T(8,128)}) custom-call(f32[32,512]{1,0:T(8,128)S(1)} %get-tuple-element.6.basis_ref, f32[32,512]{1,0:T(8,128)S(1)} %get-tuple-element.7.coimage_ref), custom_call_target="tpu_custom_call" | custom-call | tf_op jit(solution)/shard_map/pallas_call | solution.py:342

commit v10 on v9

--- a/solution.py
+++ b/solution.py
@@ -108,6 +108,7 @@
     pair = 2 * spot + other
     offsets = sorted(range(1, spots), key=lambda o: -min(o, spots - o))
     line = [lax.rem(spot + o, spots) for o in offsets]
+    arrivals = line[:1] + line[:0:-1]
     cam_peers = [lax.rem(cam + o, cams) for o in range(1, cams)]
     duo, core = proj // 2, lax.rem(proj, 2)
     sibling = 2 * duo + 1 - core
@@ -176,13 +177,13 @@
                 load.wait()
 
         total = sketched(cam)
-        for s in reversed(line):
+        for s in arrivals:
             wait_panel(2 * s + side)
             share(2 * s + side, pair, 2 * s + other)
             total += sketched(2 * s + side)
         wait_panel(pair)
         total += sketched(pair)
-        for s in reversed(line):
+        for s in arrivals:
             wait_panel(2 * s + other)
             total += sketched(2 * s + other)
         partials[step, core] = total

time: 54 us -> 53.7 us (level)
  no operation moved by 1% of the time
where the time goes in v10:
time: 53.7 us; the launch traced here: 53.5 us
  Pallas kernels  52.8 us (98%)
  between operations  0.64 us (1%)
    pallas_call x1, Pallas kernels, with_kernel(): pl.pallas_call(functools.partial(kernel, cams, projs), out_shape=kept, in...  52.2 us

profile of v10, /device:TPU:0, one launch (start us, length us, event | category | flops | bytes accessed | tf_op | source)
XLA Modules:
  0.0 53.5 jit_solution(5387004623623286084)
XLA Ops:
  0.6 52.2 %shard_map.41 = (f32[32,512]{1,0:T(8,128)S(1)}, f32[32,512]{1,0:T(8,128)S(1)}) custom-call(bf16[512,4096]{1,0:T(8,128)(2,1)} %transport_ref.1, bf16[32,512]{1,0:T(8,128)(2,1)} %bitcast.3), custom_call_target="tpu_custom_call" | custom-call | flops 536870912 | bytes 4194304 | tf_op jit(solution)/shard_map/pallas_call | solution.py:305
  52.8 0.7 %shard_map.42 = (f32[32,512]{1,0:T(8,128)}, f32[32,512]{1,0:T(8,128)}) custom-call(f32[32,512]{1,0:T(8,128)S(1)} %get-tuple-element.6.basis_ref, f32[32,512]{1,0:T(8,128)S(1)} %get-tuple-element.7.coimage_ref), custom_call_target="tpu_custom_call" | custom-call | tf_op jit(solution)/shard_map/pallas_call | solution.py:343
